TPU v7x, 128 devices: a whole 4x4x4 slice. The times are simulated.
128 devices in a mesh: cells: 16 (over z, y_lo, core), snap: 8 (over y_hi, x).
Axes of the slice: x: 4, y: 4 (y_hi: 2, y_lo: 2; y = y_hi * 2 + y_lo), z: 4, core: 2. Of those that a mesh axis runs over, the one named last changes fastest.
Arguments:
- snapshots: bfloat16 [4096, 65536], P('snap', 'cells'), may hold values from -8 to 8
- pod_basis: bfloat16 [96, 65536], P(None, 'cells'), may hold values from -0.0234375 to 0.0234375
- reference_field: bfloat16 [65536], P('cells'), may hold values from -6 to 6
- ridge_weights: float32 [4752], replicated, may hold values from 0.2 to 2
Outputs:
- trailing_gram: float32 [4752, 4752], P('cells', 'snap')
- panel_factor: float32 [4752, 512], P('cells')
All inputs are finite; a program needn't handle non-finite values.
Results may differ from a plain program's by a relative error of at most 0.0003.
Values sent between devices are 32-bit elements; how exact they have to be, the bound alone decides.
No kernel may reach another device: no remote copies, remote signals or barrier semaphores. Data moves between devices by JAX's collectives and lax.ppermute only.
A program may use at most 128 MiB of HBM per device.

v0:
```python
import functools
import jax
import jax.numpy as jnp
import numpy as np
from jax import lax
from jax.experimental import pallas as pl
from jax.experimental.pallas import tpu as pltpu
from jax.sharding import PartitionSpec as P

PANEL = 512
HALF = 256
BLOCK = 128
STEP = 32
CHUNKS = 16
SLOTS = 112
HI = lax.Precision.HIGHEST
F32 = jnp.float32
BF16 = jnp.bfloat16
NT = (((1,), (1,)), ((), ()))
TN = (((0,), (0,)), ((), ()))
NN = (((1,), (0,)), ((), ()))


def dot(a, b, dims, precision=None):
    return lax.dot_general(a, b, dims, precision=precision, preferred_element_type=F32)


def split(value):
    high = value.astype(BF16)
    return high, (value - high.astype(F32)).astype(BF16)


def dot3(a, b):
    ah, al = a
    bh, bl = b
    return dot(jnp.concatenate([ah, ah, al], 1), jnp.concatenate([bh, bl, bh], 1), NT)


def pick_tables(first, rows, modes):
    index = first + lax.broadcasted_iota(jnp.int32, (rows, 128), 0)
    slot = lax.broadcasted_iota(jnp.int32, (rows, 128), 1)

    def offset(a):
        return modes + modes * a - (a * (a - 1)) // 2

    linear = index < modes
    here = (index >= offset(slot)) & (index < offset(slot + 1)) & (slot < modes)
    right_value = jnp.where(here, index - offset(slot) + slot, 0).astype(F32)
    right_index = jnp.sum(right_value, axis=1, keepdims=True).astype(jnp.int32)
    left_index = jnp.sum(jnp.where(here, slot, 0).astype(F32), axis=1, keepdims=True).astype(jnp.int32)
    left_index = jnp.where(linear, index, left_index)
    right_index = jnp.where(linear, modes, right_index)
    return (slot == left_index).astype(F32), (slot == right_index).astype(F32)


def pick_kernel(modes, scal, lr, rr, lc, rc):
    for ref_l, ref_r, first in ((lr, rr, scal[0]), (lc, rc, scal[1])):
        rows = ref_l.shape[0]
        left, right = pick_tables(first, rows, modes)
        for ref, value in ((ref_l, left), (ref_r, right)):
            ref[:, 0:SLOTS] = value[:, 0:SLOTS].astype(BF16)
            ref[:, SLOTS : 2 * SLOTS] = value[:, 0:SLOTS].astype(BF16)


def picks(scal, row_pad, col_pad, modes):
    shapes = [(row_pad, 2 * SLOTS)] * 2 + [(col_pad, 2 * SLOTS)] * 2
    return pl.pallas_call(
        functools.partial(pick_kernel, modes),
        in_specs=[pl.BlockSpec(memory_space=pltpu.SMEM)],
        out_shape=[jax.ShapeDtypeStruct(s, BF16) for s in shapes],
        compiler_params=pltpu.CompilerParams(vmem_limit_bytes=40 * 2**20),
        name="picks",
    )(scal)


def panel_features(c_ref, t, f_ref, modes):
    f_ref[0:modes, :] = c_ref[t]
    at, a = modes, 0
    while at < PANEL:
        count = min(modes - a, PANEL - at)
        f_ref[at : at + count, :] = c_ref[t, a : a + count, :] * c_ref[t, a : a + 1, :]
        at += count
        a += 1


def corner_chunk(t, scal, own, oth, c_s, f_s, fh, fl, a_s, modes):
    g, side = t // 2, t % 2
    place = g ^ scal[2]
    place = ((place >> 2) & 1) + (place & 2) + ((place & 1) << 2)
    mine = side == scal[3]
    c_s[t] = jnp.where(mine, own[place], oth[place])
    panel_features(c_s, t, f_s, modes)
    h, l = split(f_s[...])
    fh[t] = h
    fl[t] = l
    a_s[0:HALF, :] += dot3((h[0:HALF], l[0:HALF]), (h, l))
    a_s[HALF:, HALF:] += dot3((h[HALF:], l[HALF:]), (h[HALF:], l[HALF:]))


def lane_bcast(x, c):
    return jnp.broadcast_to(x[:, c : c + 1], (8, 128))


def sub_bcast(x, k):
    return jnp.broadcast_to(x[k : k + 1, :], (8, 128))


def factor_micro(T, b, q):
    sub = lax.broadcasted_iota(jnp.int32, (8, 128), 0)
    B = {(r, k): lane_bcast(T[r][0], STEP * b + 8 * q + k) for r in range(q, 4) for k in range(8)}
    scale = None
    for k in range(8):
        rs = lax.rsqrt(sub_bcast(B[q, k], k))
        inv = rs * rs
        scale = rs if scale is None else jnp.where(sub == k, rs, scale)
        row = [sub_bcast(part, k) for part in T[q]]
        pivots = {j: sub_bcast(B[q, j], k) for j in range(k + 1, 8)}
        for r in range(q, 4):
            m = B[r, k] * inv
            if r == q:
                m = jnp.where(sub > k, m, 0.0)
            for j in range(k + 1, 8):
                B[r, j] = B[r, j] - m * pivots[j]
            T[r] = [part - m * line for part, line in zip(T[r], row)]
    T[q] = [part * scale for part in T[q]]


def factor_step(s_ref, b, between):
    lo = STEP * b
    T = [[s_ref[lo + 8 * r : lo + 8 * r + 8, 0:128], s_ref[lo + 8 * r : lo + 8 * r + 8, 128:256]] for r in range(4)]
    for q in range(4):
        factor_micro(T, b, q)
        between(4 * b + q)
    for r in range(4):
        s_ref[lo + 8 * r : lo + 8 * r + 8, 0:128] = T[r][0]
        s_ref[lo + 8 * r : lo + 8 * r + 8, 128:256] = T[r][1]
    if b < 3:
        full = s_ref[lo : lo + STEP, :]
        upd = dot(s_ref[lo : lo + STEP, 0:128], full, TN, HI)
        s_ref[lo + STEP : 128, :] -= upd[lo + STEP :, :]


def factor_block(k, a_s, s_ref, u_s, inv_s, between):
    ri = lax.broadcasted_iota(jnp.int32, (BLOCK, BLOCK), 0)
    ci = lax.broadcasted_iota(jnp.int32, (BLOCK, BLOCK), 1)
    s_ref[:, 0:BLOCK] = a_s[0:BLOCK, 0:BLOCK]
    s_ref[:, BLOCK:] = (ri == ci).astype(F32)
    for b in range(4):
        factor_step(s_ref, b, between)
    inverse = s_ref[:, BLOCK:]
    inv_s[k] = inverse
    rest = dot(inverse, a_s[0:BLOCK, BLOCK:], NN, HI)
    u_s[k, :, 0:BLOCK] = jnp.where(ci >= ri, s_ref[:, 0:BLOCK], 0.0)
    u_s[k, :, BLOCK:] = rest
    left = a_s[BLOCK:, BLOCK:] - dot(rest, rest, TN, HI)
    a_s[0 : PANEL - BLOCK, 0 : PANEL - BLOCK] = left


def stacked(c, modes):
    n = c.shape[1]
    high, low = split(c)
    gap = lax.broadcasted_iota(jnp.int32, (SLOTS - modes, n), 0)
    ones = (gap == 0).astype(F32).astype(BF16)
    none = jnp.zeros((SLOTS - modes, n), BF16)
    return jnp.concatenate([high, ones, low, none], axis=0)


def picked(left, right, cs):
    return split(dot(left, cs, NN) * dot(right, cs, NN))


def block_parts(t, c_s, fh, fl, lr, rr, lc, rc, gr, gc, gt, modes):
    env = {}

    def part0():
        cs = stacked(c_s[t], modes)
        env["fr"] = picked(lr[...], rr[...], cs)
        env["fc"] = picked(lc[...], rc[...], cs)
        env["fp"] = (fh[t], fl[t])

    def part1():
        gr[...] += dot3(env["fr"], env["fp"])

    def part2():
        gc[...] += dot3(env["fc"], env["fp"])

    def part3():
        gt[...] += dot3(env["fr"], env["fc"])

    return [part0, part1, part2, part3]


def solve_rows(g, u_s, inv_s, p_ref):
    for k in range(4):
        lo = BLOCK * k
        value = g[:, lo : lo + BLOCK]
        for j in range(k):
            off = lo - BLOCK * j
            value = value - dot(p_ref[:, BLOCK * j : BLOCK * j + BLOCK], u_s[j, :, off : off + BLOCK], NN, HI)
        p_ref[:, lo : lo + BLOCK] = dot(value, inv_s[k], NT, HI)


def main_kernel(modes, snap_total, scal, own, oth, lr, rr, lc, rc, ridge_panel, ridge_cols,
                tile_out, rows_out,
                c_s, f_s, fh, fl, a_s, s_s, u_s, inv_s, gr, gc, gt, pr, pc):
    a_s[...] = jnp.zeros_like(a_s)
    gr[...] = jnp.zeros_like(gr)
    gc[...] = jnp.zeros_like(gc)
    gt[...] = jnp.zeros_like(gt)

    def corner_body(t, carry):
        corner_chunk(t, scal, own, oth, c_s, f_s, fh, fl, a_s, modes)
        return carry

    lax.fori_loop(0, CHUNKS, corner_body, 0)
    ri = lax.broadcasted_iota(jnp.int32, (PANEL, PANEL), 0)
    ci = lax.broadcasted_iota(jnp.int32, (PANEL, PANEL), 1)
    a_s[...] = a_s[...] * (1.0 / snap_total) + jnp.where(ri == ci, ridge_panel[...], 0.0)

    def parts_of(t):
        return block_parts(t, c_s, fh, fl, lr, rr, lc, rc, gr, gc, gt, modes)

    def block_body(k, carry):
        parts = []
        for b in range(4):
            parts += parts_of(4 * k + b)
        factor_block(k, a_s, s_s, u_s, inv_s, lambda i: parts[i]())
        return carry

    lax.fori_loop(0, 4, block_body, 0)

    first_row, first_col = scal[0], scal[1]
    inv_total = 1.0 / snap_total
    for g, p, first in ((gr, pr, first_row), (gc, pc, first_col)):
        rows = g.shape[0]
        ri = first + lax.broadcasted_iota(jnp.int32, (rows, PANEL), 0)
        ci = lax.broadcasted_iota(jnp.int32, (rows, PANEL), 1)
        g[...] = g[...] * inv_total + jnp.where(ri == ci, ridge_panel[...], 0.0)
        solve_rows(g, u_s, inv_s, p)

    rows, cols = tile_out.shape
    total = gt[...] * inv_total
    ri = first_row + lax.broadcasted_iota(jnp.int32, total.shape, 0)
    ci = first_col + lax.broadcasted_iota(jnp.int32, total.shape, 1)
    total = total + jnp.where(ri == ci, ridge_cols[...], 0.0)
    update = dot3(split(pr[...]), split(pc[...]))
    total = jnp.where((ri >= PANEL) & (ci >= PANEL), total - update, total)
    tile_out[...] = total[0:rows, 0:cols]
    line = first_row + lax.broadcasted_iota(jnp.int32, (rows, PANEL), 0)
    at = lax.broadcasted_iota(jnp.int32, (rows, PANEL), 1)
    rows_out[...] = jnp.where(at <= line, pr[0:rows, :], 0.0)


def main(scal, own, oth, tables, ridge_panel, ridge_cols, rows, cols, snap_total):
    modes = own.shape[1]
    n = own.shape[2]
    lr, rr, lc, rc = tables
    row_pad, col_pad = lr.shape[0], lc.shape[0]
    vmem = pl.BlockSpec(memory_space=pltpu.VMEM)
    return pl.pallas_call(
        functools.partial(main_kernel, modes, snap_total),
        in_specs=[pl.BlockSpec(memory_space=pltpu.SMEM)] + [vmem] * 8,
        out_specs=[vmem, vmem],
        out_shape=[jax.ShapeDtypeStruct((rows, cols), F32), jax.ShapeDtypeStruct((rows, PANEL), F32)],
        scratch_shapes=[
            pltpu.VMEM((CHUNKS, modes, n), F32),
            pltpu.VMEM((PANEL, n), F32),
            pltpu.VMEM((CHUNKS, PANEL, n), BF16),
            pltpu.VMEM((CHUNKS, PANEL, n), BF16),
            pltpu.VMEM((PANEL, PANEL), F32),
            pltpu.VMEM((BLOCK, 2 * BLOCK), F32),
            pltpu.VMEM((4, BLOCK, PANEL), F32),
            pltpu.VMEM((4, BLOCK, BLOCK), F32),
            pltpu.VMEM((row_pad, PANEL), F32),
            pltpu.VMEM((col_pad, PANEL), F32),
            pltpu.VMEM((row_pad, col_pad), F32),
            pltpu.VMEM((row_pad, PANEL), F32),
            pltpu.VMEM((col_pad, PANEL), F32),
        ],
        compiler_params=pltpu.CompilerParams(vmem_limit_bytes=60 * 2**20),
        name="gram_factor",
    )(scal, own, oth, lr, rr, lc, rc, ridge_panel, ridge_cols)


def swap(value, axis, bit):
    size = lax.axis_size(axis)
    return lax.ppermute(value, axis, [(i, i ^ bit) for i in range(size)])


def gather_coeffs(partial, core):
    half = partial.shape[1] // 2
    keep = lax.dynamic_slice_in_dim(partial, core * half, half, 1)
    send = lax.dynamic_slice_in_dim(partial, (1 - core) * half, half, 1)
    total = keep + swap(send, "cells", 1)
    for bit in (2, 4, 8):
        total = total + swap(total, "cells", bit)
    blocks = total[None]
    for bit in (4, 2, 1):
        blocks = jnp.concatenate([blocks, swap(blocks, "snap", bit)], axis=0)
    return blocks, swap(blocks, "cells", 1)


def padded(count):
    return -(-count // 16) * 16


def per_device(snapshots, pod_basis, reference_field, ridge_weights):
    contract = (((1,), (1,)), ((), ()))
    modes = pod_basis.shape[0]
    snap_total = snapshots.shape[0] * lax.axis_size("snap")
    feature_total = ridge_weights.shape[0]
    rows = feature_total // lax.axis_size("cells")
    cols = feature_total // lax.axis_size("snap")
    group = lax.axis_index("snap")
    core = lax.axis_index("cells") & 1
    first_row = lax.axis_index("cells") * rows
    first_col = group * cols
    scal = jnp.stack([first_row, first_col, group, core]).astype(jnp.int32)
    tables = picks(scal, padded(rows), padded(cols), modes)
    ridge_panel = ridge_weights[None, :PANEL]
    ridge_cols = lax.dynamic_slice_in_dim(ridge_weights, first_col, cols)
    ridge_cols = jnp.pad(ridge_cols, (0, padded(cols) - cols))[None, :]

    projected = lax.dot_general(pod_basis, snapshots, contract, preferred_element_type=F32)
    offset = lax.dot_general(pod_basis, reference_field[None, :], contract, preferred_element_type=F32)
    own, other = gather_coeffs(projected - offset, core)
    return tuple(main(scal, own, other, tables, ridge_panel, ridge_cols, rows, cols, snap_total))


def solution(mesh):
    return jax.shard_map(
        per_device,
        mesh=mesh,
        in_specs=(P("snap", "cells"), P(None, "cells"), P("cells"), P()),
        out_specs=(P("cells", "snap"), P("cells", None)),
        check_vma=False,
    )
```

profile of v0, /device:TPU:1, one launch (start us, length us, event | category | flops | bytes accessed | tf_op | source)
XLA Modules:
  0.0 101.2 jit_solution(2138976328370722924)
XLA Ops:
  0.7 0.8 reshape.8
  2.1 3.6 %convolution_subtract_fusion = f32[96,512]{1,0:T(8,128)S(1)} fusion(bf16[96,4096]{1,0:T(8,128)(2,1)S(1)} %copy-done, bf16[512,4096]{1,0:T(8,128)(2,1)} %param.4, f32[96]{0:T(128)S(1)} %convolution_bitcast_fusion), kind=kOutput, calls=%fused_computation | convolution fusion | flops 402702336 | bytes 5177728 | tf_op jit(solution)/shard_map/dot_general | solution.py:324
  5.7 1.5 %collective-permute-start = (f32[96,256]{1,0:T(8,128)S(1)}, f32[96,256]{1,0:T(8,128)S(1)}, u32[]{:S(2)}, u32[]{:S(2)}) collective-permute-start(f32[96,256]{1,0:T(8,128)S(1)} %constant_dynamic-slice_fusion), channel_id=1, source_target_pairs={{0,8},{8,0},{16,24},{24,16},{32,40},{40,32},{48,56},{56,48},{64,72... | collective-permute-start | bytes 294920 | tf_op jit(solution)/shard_map/ppermute | solution.py:287
  7.2 0.9 collective-permute-done
  8.2 1.5 %collective-permute-start.1 = (f32[96,256]{1,0:T(8,128)S(1)}, f32[96,256]{1,0:T(8,128)S(1)}, u32[]{:S(2)}, u32[]{:S(2)}) collective-permute-start(f32[96,256]{1,0:T(8,128)S(1)} %dynamic-slice_add_fusion), channel_id=1, source_target_pairs={{0,16},{8,24},{16,0},{24,8},{32,48},{40,56},{48,32},{56,40},{64,80... | collective-permute-start | bytes 294920 | tf_op jit(solution)/shard_map/ppermute | solution.py:287
  9.7 2.6 %collective-permute-done.1 = f32[96,256]{1,0:T(8,128)S(1)} collective-permute-done((f32[96,256]{1,0:T(8,128)S(1)}, f32[96,256]{1,0:T(8,128)S(1)}, u32[]{:S(2)}, u32[]{:S(2)}) %collective-permute-start.1) | collective-permute-done | bytes 98336 | tf_op jit(solution)/shard_map/ppermute | solution.py:287
  12.3 1.8 %collective-permute-start.2 = (f32[96,256]{1,0:T(8,128)S(1)}, f32[96,256]{1,0:T(8,128)S(1)}, u32[]{:S(2)}, u32[]{:S(2)}) collective-permute-start(f32[96,256]{1,0:T(8,128)S(1)} %add.26), channel_id=1, source_target_pairs={{0,32},{8,40},{16,48},{24,56},{32,0},{40,8},{48,16},{56,24},{64,96... | collective-permute-start | bytes 294920 | tf_op jit(solution)/shard_map/ppermute | solution.py:287
  14.1 2.0 %collective-permute-done.2 = f32[96,256]{1,0:T(8,128)S(1)} collective-permute-done((f32[96,256]{1,0:T(8,128)S(1)}, f32[96,256]{1,0:T(8,128)S(1)}, u32[]{:S(2)}, u32[]{:S(2)}) %collective-permute-start.2) | collective-permute-done | bytes 98336 | tf_op jit(solution)/shard_map/ppermute | solution.py:287
  16.2 3.5 %collective-permute-start.3 = (f32[96,256]{1,0:T(8,128)S(1)}, f32[96,256]{1,0:T(8,128)S(1)}, u32[]{:S(2)}, u32[]{:S(2)}) collective-permute-start(f32[96,256]{1,0:T(8,128)S(1)} %add.27), channel_id=1, source_target_pairs={{0,64},{8,72},{16,80},{24,88},{32,96},{40,104},{48,112},{56,120},{... | collective-permute-start | bytes 294920 | tf_op jit(solution)/shard_map/ppermute | solution.py:287
  19.7 2.5 %collective-permute-done.3 = f32[96,256]{1,0:T(8,128)S(1)} collective-permute-done((f32[96,256]{1,0:T(8,128)S(1)}, f32[96,256]{1,0:T(8,128)S(1)}, u32[]{:S(2)}, u32[]{:S(2)}) %collective-permute-start.3) | collective-permute-done | bytes 98336 | tf_op jit(solution)/shard_map/ppermute | solution.py:287
  22.1 3.0 %collective-permute-start.4 = (f32[1,96,256]{2,1,0:T(8,128)S(1)}, f32[1,96,256]{2,1,0:T(8,128)S(1)}, u32[]{:S(2)}, u32[]{:S(2)}) collective-permute-start(f32[1,96,256]{2,1,0:T(8,128)S(1)} %add_bitcast_fusion), channel_id=1, source_target_pairs={{0,4},{1,5},{2,6},{3,7},{4,0},{5,1},{6,2},{7,3},{8,12},{9,13},{10,... | collective-permute-start | bytes 294920 | tf_op jit(solution)/shard_map/ppermute | solution.py:287
  25.1 2.1 %collective-permute-done.4 = f32[1,96,256]{2,1,0:T(8,128)S(1)} collective-permute-done((f32[1,96,256]{2,1,0:T(8,128)S(1)}, f32[1,96,256]{2,1,0:T(8,128)S(1)}, u32[]{:S(2)}, u32[]{:S(2)}) %collective-permute-start.4) | collective-permute-done | bytes 98336 | tf_op jit(solution)/shard_map/ppermute | solution.py:287
  27.2 2.8 %collective-permute-start.5 = (f32[2,96,256]{2,1,0:T(8,128)S(1)}, f32[2,96,256]{2,1,0:T(8,128)S(1)}, u32[]{:S(2)}, u32[]{:S(2)}) collective-permute-start(f32[2,96,256]{2,1,0:T(8,128)S(1)} %pad_maximum_fusion.2), channel_id=1, source_target_pairs={{0,2},{1,3},{2,0},{3,1},{4,6},{5,7},{6,4},{7,5},{8,10},{9,11},{10,... | collective-permute-start | bytes 589832 | tf_op jit(solution)/shard_map/ppermute | solution.py:287
  30.0 3.3 %collective-permute-done.5 = f32[2,96,256]{2,1,0:T(8,128)S(1)} collective-permute-done((f32[2,96,256]{2,1,0:T(8,128)S(1)}, f32[2,96,256]{2,1,0:T(8,128)S(1)}, u32[]{:S(2)}, u32[]{:S(2)}) %collective-permute-start.5) | collective-permute-done | bytes 196640 | tf_op jit(solution)/shard_map/ppermute | solution.py:287
  33.4 1.3 %collective-permute-start.6 = (f32[4,96,256]{2,1,0:T(8,128)S(1)}, f32[4,96,256]{2,1,0:T(8,128)S(1)}, u32[]{:S(2)}, u32[]{:S(2)}) collective-permute-start(f32[4,96,256]{2,1,0:T(8,128)S(1)} %pad_maximum_fusion.1), channel_id=1, source_target_pairs={{0,1},{1,0},{2,3},{3,2},{4,5},{5,4},{6,7},{7,6},{8,9},{9,8},{10,11... | collective-permute-start | bytes 1179656 | tf_op jit(solution)/shard_map/ppermute | solution.py:287
  34.6 7.3 %collective-permute-done.6 = f32[4,96,256]{2,1,0:T(8,128)S(1)} collective-permute-done((f32[4,96,256]{2,1,0:T(8,128)S(1)}, f32[4,96,256]{2,1,0:T(8,128)S(1)}, u32[]{:S(2)}, u32[]{:S(2)}) %collective-permute-start.6) | collective-permute-done | bytes 393248 | tf_op jit(solution)/shard_map/ppermute | solution.py:287
  42.1 5.2 %collective-permute-start.7 = (f32[8,96,256]{2,1,0:T(8,128)S(1)}, f32[8,96,256]{2,1,0:T(8,128)S(1)}, u32[]{:S(2)}, u32[]{:S(2)}) collective-permute-start(f32[8,96,256]{2,1,0:T(8,128)S(1)} %pad_maximum_fusion.own), channel_id=1, source_target_pairs={{0,8},{8,0},{16,24},{24,16},{32,40},{40,32},{48,56},{56,48},{64,72... | collective-permute-start | bytes 2359304 | tf_op jit(solution)/shard_map/ppermute | solution.py:287
  47.3 1.3 %slice.3 = f32[512]{0:T(512)} slice(f32[4752]{0:T(1024)} %param.7), slice={[0:512]} | slice | bytes 4096 | tf_op jit(solution)/shard_map/slice | solution.py:320
  48.6 0.8 dynamic_slice.11
  50.0 1.2 %picks.1 = (bf16[304,224]{1,0:T(8,128)(2,1)S(1)}, bf16[304,224]{1,0:T(8,128)(2,1)S(1)}, bf16[608,224]{1,0:T(8,128)(2,1)S(1)}, bf16[608,224]{1,0:T(8,128)(2,1)S(1)}) custom-call(s32[4]{0:T(128)S(1)} %pad_add_fusion.scal), custom_call_target="tpu_custom_call" | custom-call | tf_op jit(solution)/shard_map/picks/pallas_call | solution.py:67
  51.2 0.7 copy-done.1
  52.0 0.7 copy-done.2
  54.0 0.9 copy-done.7
  54.9 46.3 %gram_factor.1 = (f32[297,594]{1,0:T(8,128)}, f32[297,512]{1,0:T(8,128)}) custom-call(s32[4]{0:T(128)} %copy-done.5, f32[8,96,256]{2,1,0:T(8,128)} %copy-done.6, f32[8,96,256]{2,1,0:T(8,128)} %copy-done.7, bf16[304,224]{1,0:T(8,128)(2,1)} %copy-done.3, bf16[304,224]{1,0:T(8,128)(2,1)} %copy-done.4, bf16[608,224]{1,0:T(8,128)(2,1)} %copy-done.1, ...), custom_call_target="tpu_custom_call" | custom-call | tf_op jit(solution)/shard_map/gram_factor/pallas_call | solution.py:260
  (26 shorter events, 2.8 us)
Async XLA Ops:
  0.6 1.2 %copy-start = (bf16[96,4096]{1,0:T(8,128)(2,1)S(1)}, bf16[96,4096]{1,0:T(8,128)(2,1)}, u32[]{:S(2)}) copy-start(bf16[96,4096]{1,0:T(8,128)(2,1)} %param.5) | copy-start | bytes 2359300
  5.7 2.4 %collective-permute-start = (f32[96,256]{1,0:T(8,128)S(1)}, f32[96,256]{1,0:T(8,128)S(1)}, u32[]{:S(2)}, u32[]{:S(2)}) collective-permute-start(f32[96,256]{1,0:T(8,128)S(1)} %constant_dynamic-slice_fusion), channel_id=1, source_target_pairs={{0,8},{8,0},{16,24},{24,16},{32,40},{40,32},{48,56},{56,48},{64,72... | collective-permute-start | bytes 294920 | tf_op jit(solution)/shard_map/ppermute | solution.py:287
  8.2 4.1 %collective-permute-start.1 = (f32[96,256]{1,0:T(8,128)S(1)}, f32[96,256]{1,0:T(8,128)S(1)}, u32[]{:S(2)}, u32[]{:S(2)}) collective-permute-start(f32[96,256]{1,0:T(8,128)S(1)} %dynamic-slice_add_fusion), channel_id=1, source_target_pairs={{0,16},{8,24},{16,0},{24,8},{32,48},{40,56},{48,32},{56,40},{64,80... | collective-permute-start | bytes 294920 | tf_op jit(solution)/shard_map/ppermute | solution.py:287
  12.3 3.8 %collective-permute-start.2 = (f32[96,256]{1,0:T(8,128)S(1)}, f32[96,256]{1,0:T(8,128)S(1)}, u32[]{:S(2)}, u32[]{:S(2)}) collective-permute-start(f32[96,256]{1,0:T(8,128)S(1)} %add.26), channel_id=1, source_target_pairs={{0,32},{8,40},{16,48},{24,56},{32,0},{40,8},{48,16},{56,24},{64,96... | collective-permute-start | bytes 294920 | tf_op jit(solution)/shard_map/ppermute | solution.py:287
  16.2 6.0 %collective-permute-start.3 = (f32[96,256]{1,0:T(8,128)S(1)}, f32[96,256]{1,0:T(8,128)S(1)}, u32[]{:S(2)}, u32[]{:S(2)}) collective-permute-start(f32[96,256]{1,0:T(8,128)S(1)} %add.27), channel_id=1, source_target_pairs={{0,64},{8,72},{16,80},{24,88},{32,96},{40,104},{48,112},{56,120},{... | collective-permute-start | bytes 294920 | tf_op jit(solution)/shard_map/ppermute | solution.py:287
  22.1 5.1 %collective-permute-start.4 = (f32[1,96,256]{2,1,0:T(8,128)S(1)}, f32[1,96,256]{2,1,0:T(8,128)S(1)}, u32[]{:S(2)}, u32[]{:S(2)}) collective-permute-start(f32[1,96,256]{2,1,0:T(8,128)S(1)} %add_bitcast_fusion), channel_id=1, source_target_pairs={{0,4},{1,5},{2,6},{3,7},{4,0},{5,1},{6,2},{7,3},{8,12},{9,13},{10,... | collective-permute-start | bytes 294920 | tf_op jit(solution)/shard_map/ppermute | solution.py:287
  27.2 6.1 %collective-permute-start.5 = (f32[2,96,256]{2,1,0:T(8,128)S(1)}, f32[2,96,256]{2,1,0:T(8,128)S(1)}, u32[]{:S(2)}, u32[]{:S(2)}) collective-permute-start(f32[2,96,256]{2,1,0:T(8,128)S(1)} %pad_maximum_fusion.2), channel_id=1, source_target_pairs={{0,2},{1,3},{2,0},{3,1},{4,6},{5,7},{6,4},{7,5},{8,10},{9,11},{10,... | collective-permute-start | bytes 589832 | tf_op jit(solution)/shard_map/ppermute | solution.py:287
  33.4 8.6 %collective-permute-start.6 = (f32[4,96,256]{2,1,0:T(8,128)S(1)}, f32[4,96,256]{2,1,0:T(8,128)S(1)}, u32[]{:S(2)}, u32[]{:S(2)}) collective-permute-start(f32[4,96,256]{2,1,0:T(8,128)S(1)} %pad_maximum_fusion.1), channel_id=1, source_target_pairs={{0,1},{1,0},{2,3},{3,2},{4,5},{5,4},{6,7},{7,6},{8,9},{9,8},{10,11... | collective-permute-start | bytes 1179656 | tf_op jit(solution)/shard_map/ppermute | solution.py:287
  42.0 12.0 %copy-start.6 = (f32[8,96,256]{2,1,0:T(8,128)}, f32[8,96,256]{2,1,0:T(8,128)S(1)}, u32[]{:S(2)}) copy-start(f32[8,96,256]{2,1,0:T(8,128)S(1)} %pad_maximum_fusion.own) | copy-start | bytes 2359300
  42.1 12.0 %collective-permute-start.7 = (f32[8,96,256]{2,1,0:T(8,128)S(1)}, f32[8,96,256]{2,1,0:T(8,128)S(1)}, u32[]{:S(2)}, u32[]{:S(2)}) collective-permute-start(f32[8,96,256]{2,1,0:T(8,128)S(1)} %pad_maximum_fusion.own), channel_id=1, source_target_pairs={{0,8},{8,0},{16,24},{24,16},{32,40},{40,32},{48,56},{56,48},{64,72... | collective-permute-start | bytes 2359304 | tf_op jit(solution)/shard_map/ppermute | solution.py:287
  50.0 4.0 %copy-start.5 = (s32[4]{0:T(128)}, s32[4]{0:T(128)S(1)}, u32[]{:S(2)}) copy-start(s32[4]{0:T(128)S(1)} %pad_add_fusion.scal) | copy-start | bytes 52
  51.2 0.7 copy-start.1
  52.0 0.7 copy-start.2
  52.7 0.7 copy-start.3
  53.4 0.7 copy-start.4
  54.0 0.9 copy-start.7
where the time goes:
time: 102 us; the launch traced here: 101 us
  Pallas kernels  47.5 us (47%)
  waiting for transfers between devices  20.7 us (20%)
  starting transfers between devices  20.6 us (20%)
  local copies, waits for them, and re-layouts  7.47 us (7%)
  matrix products  3.93 us (4%)
    pallas_call x1, Pallas kernels, main(): pl.pallas_call(functools.partial(main_kernel, modes, snap_total), in_spec...  46.3 us
    ppermute x8, waiting for transfers between devices, swap(): return lax.ppermute(value, axis, [(i, i ^ bit) for i in range(size)])  20.7 us
    ppermute x8, starting transfers between devices, swap(): return lax.ppermute(value, axis, [(i, i ^ bit) for i in range(size)])  20.6 us
    unnamed x17, local copies, waits for them, and re-layouts  4.81 us
    dot_general x1, matrix products, per_device(): lax.dot_general(pod_basis, snapshots, contract, preferred_element_type=F32)  3.63 us
  transfers between devices with their start and end apart: 8, of which 7 were waited for; matrix products, arithmetic and copies ran while one was open for 3% of the time, Pallas kernels for 1%

commit v1 on v0

v1 whole, which is shorter than its diff:
```python
import functools
import jax
import jax.numpy as jnp
import numpy as np
from jax import lax
from jax.experimental import pallas as pl
from jax.experimental.pallas import tpu as pltpu
from jax.sharding import PartitionSpec as P

PANEL = 512
HALF = 256
BLOCK = 128
STEP = 32
SLOTS = 112
F32 = jnp.float32
BF16 = jnp.bfloat16
NT = (((1,), (1,)), ((), ()))
TN = (((0,), (0,)), ((), ()))
NN = (((1,), (0,)), ((), ()))


def dot(a, b, dims, precision=None):
    return lax.dot_general(a, b, dims, precision=precision, preferred_element_type=F32)


def split(value):
    high = value.astype(BF16)
    return high, (value - high.astype(F32)).astype(BF16)


def dot3(a, b):
    ah, al = a
    bh, bl = b
    return dot(jnp.concatenate([ah, ah, al], 1), jnp.concatenate([bh, bl, bh], 1), NT)


def pick_tables(first, rows, modes):
    index = first + lax.broadcasted_iota(jnp.int32, (rows, 128), 0)
    slot = lax.broadcasted_iota(jnp.int32, (rows, 128), 1)

    def offset(a):
        return modes + modes * a - (a * (a - 1)) // 2

    linear = index < modes
    here = (index >= offset(slot)) & (index < offset(slot + 1)) & (slot < modes)
    right_value = jnp.where(here, index - offset(slot) + slot, 0).astype(F32)
    right_index = jnp.sum(right_value, axis=1, keepdims=True).astype(jnp.int32)
    left_index = jnp.sum(jnp.where(here, slot, 0).astype(F32), axis=1, keepdims=True).astype(jnp.int32)
    left_index = jnp.where(linear, index, left_index)
    right_index = jnp.where(linear, modes, right_index)
    return (slot == left_index).astype(F32), (slot == right_index).astype(F32)


def pick_kernel(modes, scale, scal, lr, rr, lc, rc):
    for ref_l, ref_r, first in ((lr, rr, scal[0]), (lc, rc, scal[1])):
        rows = ref_l.shape[0]
        left, right = pick_tables(first, rows, modes)
        left = left * scale
        for ref, value in ((ref_l, left), (ref_r, right)):
            ref[:, 0:SLOTS] = value[:, 0:SLOTS].astype(BF16)
            ref[:, SLOTS : 2 * SLOTS] = value[:, 0:SLOTS].astype(BF16)


def picks(scal, row_pad, col_pad, modes, scale):
    shapes = [(row_pad, 2 * SLOTS)] * 2 + [(col_pad, 2 * SLOTS)] * 2
    return pl.pallas_call(
        functools.partial(pick_kernel, modes, scale),
        in_specs=[pl.BlockSpec(memory_space=pltpu.SMEM)],
        out_shape=[jax.ShapeDtypeStruct(s, BF16) for s in shapes],
        compiler_params=pltpu.CompilerParams(vmem_limit_bytes=40 * 2**20),
        name="picks",
    )(scal)


def panel_features(c_ref, t, f_ref, modes, scale):
    f_ref[0:modes, :] = c_ref[t] * scale
    at, a = modes, 0
    while at < PANEL:
        count = min(modes - a, PANEL - at)
        f_ref[at : at + count, :] = c_ref[t, a : a + count, :] * (c_ref[t, a : a + 1, :] * scale)
        at += count
        a += 1


def panel_pair(t, c_s, f_s, fh, fl, modes, scale):
    for i in range(2):
        panel_features(c_s, t + i, f_s.at[i], modes, scale)
        fh[t + i], fl[t + i] = split(f_s[i])


def corner_pair(t, fh, fl, a_ref):
    pairs = [(fh[t + i], fl[t + i]) for i in range(2)]
    top = [dot3((h[0:HALF], l[0:HALF]), (h, l)) for h, l in pairs]
    low = [dot3((h[HALF:], l[HALF:]), (h[HALF:], l[HALF:])) for h, l in pairs]
    a_ref[0:HALF, :] = top[0] + top[1]
    a_ref[HALF:, HALF:] = low[0] + low[1]


def lane_bcast(x, c):
    return jnp.broadcast_to(x[:, c : c + 1], (8, 128))


def sub_bcast(x, k):
    return jnp.broadcast_to(x[k : k + 1, :], (8, 128))


def split3(value):
    high = value.astype(BF16)
    rest = value - high.astype(F32)
    middle = rest.astype(BF16)
    return high, middle, (rest - middle.astype(F32)).astype(BF16)


def update_dot(left, right):
    lh, lm, ll = split3(left)
    rh, rm, rl = split3(right)
    return dot(
        jnp.concatenate([lh, lh, lh, lm, lm, ll], 0), jnp.concatenate([rh, rm, rl, rh, rm, rh], 0), TN
    )


def dot_split(a, b, dims):
    ah, al = a
    bh, bl = b
    return dot(ah, bh, dims) + (dot(ah, bl, dims) + dot(al, bh, dims))


def factor_step(s_ref, b, between):
    lo = STEP * b
    strips = STEP // 8
    sub = lax.broadcasted_iota(jnp.int32, (8, 128), 0)
    T = [[s_ref[lo + 8 * r : lo + 8 * r + 8, 0:128], s_ref[lo + 8 * r : lo + 8 * r + 8, 128:256]] for r in range(strips)]
    B = {(r, j): lane_bcast(T[r][0], lo + j) for j in range(STEP) for r in range(j // 8, strips)}
    for q in range(strips):
        scale = None
        for k in range(8 * q, 8 * q + 8):
            rs = lax.rsqrt(sub_bcast(B[q, k], k - 8 * q))
            inv = rs * rs
            scale = rs if scale is None else jnp.where(sub == k - 8 * q, rs, scale)
            row = [sub_bcast(part, k - 8 * q) for part in T[q]]
            pivots = {j: sub_bcast(B[j // 8, k], j % 8) for j in range(k + 1, STEP)}
            for r in range(q, strips):
                m = B[r, k] * inv
                if r == q:
                    m = jnp.where(sub > k - 8 * q, m, 0.0)
                for j in range(k + 1, STEP):
                    if j // 8 <= r:
                        B[r, j] = B[r, j] - m * pivots[j]
                T[r] = [part - m * line for part, line in zip(T[r], row)]
        T[q] = [part * scale for part in T[q]]
        between(4 * b + q)
    for r in range(strips):
        s_ref[lo + 8 * r : lo + 8 * r + 8, 0:128] = T[r][0]
        s_ref[lo + 8 * r : lo + 8 * r + 8, 128:256] = T[r][1]
    if b < 3:
        full = s_ref[lo : lo + STEP, :]
        upd = update_dot(full[:, 0:128], full)
        s_ref[lo + STEP : 128, :] -= upd[lo + STEP :, :]


def factor_block(k, a_s, s_ref, e_s, u_s, inv_s, low_s, between):
    ri = lax.broadcasted_iota(jnp.int32, (BLOCK, BLOCK), 0)
    ci = lax.broadcasted_iota(jnp.int32, (BLOCK, BLOCK), 1)
    s_ref[:, 0:BLOCK] = a_s[0:BLOCK, 0:BLOCK]
    s_ref[:, BLOCK:] = (ri == ci).astype(F32)
    for b in range(4):
        factor_step(s_ref, b, between)
    inverse = s_ref[:, BLOCK:]
    inv_s[k] = inverse
    inv_parts = split(inverse)
    rest = dot_split(inv_parts, split(a_s[0:BLOCK, BLOCK:]), NN)
    parts = split(rest)
    a_s[0 : PANEL - BLOCK, 0 : PANEL - BLOCK] = a_s[BLOCK:, BLOCK:] - dot_split(parts, parts, TN)
    u_s[k, :, 0:BLOCK] = jnp.where(ci >= ri, s_ref[:, 0:BLOCK], 0.0)
    u_s[k, :, BLOCK:] = rest
    low_s[k] = dot_split(inv_parts, split(e_s[...]), NN)
    e_s[...] = -dot_split((parts[0][:, 0:BLOCK], parts[1][:, 0:BLOCK]), inv_parts, TN)


def stacked(c, modes):
    n = c.shape[1]
    high, low = split(c)
    gap = lax.broadcasted_iota(jnp.int32, (SLOTS - modes, n), 0)
    ones = (gap == 0).astype(F32).astype(BF16)
    none = jnp.zeros((SLOTS - modes, n), BF16)
    return jnp.concatenate([high, ones, low, none], axis=0)


def picked(left, right, cs):
    return split(dot(left, cs, NN) * dot(right, cs, NN))


def block_parts(t, c_s, fh, fl, lr, rr, lc, rc, gr, gc, gt, modes):
    env = {}

    def part0():
        cs = stacked(c_s[t], modes)
        env["fr"] = picked(lr[...], rr[...], cs)
        env["fc"] = picked(lc[...], rc[...], cs)
        env["fp"] = (fh[t], fl[t])

    def part1():
        gr[...] += dot3(env["fr"], env["fp"])

    def part2():
        gc[...] += dot3(env["fc"], env["fp"])

    def part3():
        gt[...] += dot3(env["fr"], env["fc"])

    return [part0, part1, part2, part3]


def pair_inverse(p, inv_s, low_s):
    zero = jnp.zeros((BLOCK, BLOCK), F32)
    top = jnp.concatenate([inv_s[2 * p], zero], 1)
    return split(jnp.concatenate([top, jnp.concatenate([low_s[2 * p + 1], inv_s[2 * p + 1]], 1)], 0))


def solve_rows(g, inverses, cross, p_ref):
    first = dot_split(split(g[:, 0:HALF]), inverses[0], NT)
    p_ref[:, 0:HALF] = first
    value = g[:, HALF:] - dot_split(split(first), cross, NN)
    p_ref[:, HALF:] = dot_split(split(value), inverses[1], NT)


def diagonal(shape, first_row, first_col, values):
    ri = first_row + lax.broadcasted_iota(jnp.int32, shape, 0)
    ci = first_col + lax.broadcasted_iota(jnp.int32, shape, 1)
    return jnp.where(ri == ci, values, 0.0)


def diagonal(shape, first_row, first_col, values):
    ri = first_row + lax.broadcasted_iota(jnp.int32, shape, 0)
    ci = first_col + lax.broadcasted_iota(jnp.int32, shape, 1)
    return jnp.where(ri == ci, values, 0.0)


def early_kernel(modes, scale, first, extra, *refs):
    own, oth, lr, rr, lc, rc = refs[0:6]
    if first:
        scal, ridge_panel, ridge_cols = refs[6:9]
        a_out, gr, gc, gt, c_s, f_s, fh, fl, a_s = refs[9:]
        gr[...] = jnp.zeros_like(gr)
        gc[...] = diagonal(gc.shape, scal[1], 0, ridge_panel[...])
        gt[...] = diagonal(gt.shape, scal[0], scal[1], ridge_cols[...])
    else:
        gr_in, gc_in, gt_in = refs[6:9]
        a_out, gr, gc, gt, c_s, f_s, fh, fl, a_s, pair_s = refs[9:]
        gc[...] = gc_in[...]
        gt[...] = gt_in[...]
        pair_s[...] = jnp.zeros_like(pair_s)
    for i in range(2):
        c_s[i] = own[i]
        c_s[2 + i] = oth[i]
    for t in (0, 2):
        panel_pair(t, c_s, f_s, fh, fl, modes, scale)
    corner_pair(0, fh, fl, a_s)
    corner_pair(2, fh, fl, a_out)
    a_out[...] += a_s[...]
    target = gr if first else pair_s
    for t in range(2):
        for part in block_parts(t, c_s, fh, fl, lr, rr, lc, rc, target, gc, gt, modes):
            part()
    if not first:
        gr[...] = gr_in[...] + pair_s[...]


def early(own, oth, tables, rest, first, modes, scale, cost):
    lr, rr, lc, rc = tables
    row_pad, col_pad = lr.shape[0], lc.shape[0]
    n = own.shape[2]
    vmem = pl.BlockSpec(memory_space=pltpu.VMEM)
    smem = pl.BlockSpec(memory_space=pltpu.SMEM)
    scratch = [
        pltpu.VMEM((4, modes, n), F32),
        pltpu.VMEM((2, PANEL, n), F32),
        pltpu.VMEM((4, PANEL, n), BF16),
        pltpu.VMEM((4, PANEL, n), BF16),
        pltpu.VMEM((PANEL, PANEL), F32),
    ]
    if not first:
        scratch.append(pltpu.VMEM((row_pad, PANEL), F32))
    shapes = [(PANEL, PANEL), (row_pad, PANEL), (col_pad, PANEL), (row_pad, col_pad)]
    return pl.pallas_call(
        functools.partial(early_kernel, modes, scale, first, False),
        in_specs=[vmem] * 6 + ([smem, vmem, vmem] if first else [vmem] * 3),
        out_specs=[vmem] * 4,
        out_shape=[jax.ShapeDtypeStruct(s, F32) for s in shapes],
        scratch_shapes=scratch,
        compiler_params=pltpu.CompilerParams(vmem_limit_bytes=32 * 2**20),
        cost_estimate=pl.CostEstimate(flops=cost, bytes_accessed=2**22, transcendentals=0),
        name="early_first" if first else "early_second",
    )(own, oth, lr, rr, lc, rc, *rest)


LATE = 12


def main_kernel(modes, scale, scal, own, oth_a, oth_b, oth, lr, rr, lc, rc, ridge_panel, a0, a1, gr_in, gc_in, gt_in,
                tile_out, rows_out,
                c_s, f_s, fh, fl, a_p, a_s, s_s, e_s, u_s, inv_s, low_s, gr, gc, gt, pr, pc):
    first_row, first_col = scal[0], scal[1]
    for i in range(4):
        c_s[i] = own[i]
        c_s[8 + i] = oth[i]
    for i in range(2):
        c_s[4 + i] = oth_a[i]
        c_s[6 + i] = oth_b[i]

    def corner_body(i, carry):
        t = 2 * (i % 2) + 8 * (i // 2)
        panel_pair(t, c_s, f_s, fh, fl, modes, scale)
        corner_pair(t, fh, fl, a_p.at[i])
        return carry

    lax.fori_loop(0, 4, corner_body, 0)
    total = (a0[...] + a1[...]) + ((a_p[0] + a_p[2]) + (a_p[1] + a_p[3]))
    a_s[...] = total + diagonal(a_s.shape, 0, 0, ridge_panel[...])
    for t in (4, 6):
        panel_pair(t, c_s, f_s, fh, fl, modes, scale)
    gr[...] = jnp.zeros_like(gr)
    gc[...] = gc_in[...]
    gt[...] = gt_in[...]
    e_s[...] = jnp.zeros_like(e_s)

    def block_body(k, carry):
        parts = []
        for b in range(3):
            t = 3 * k + b
            parts += block_parts(t, c_s, fh, fl, lr, rr, lc, rc, gr.at[t // 2], gc, gt, modes)
        slots = [[] for _ in range(16)]
        for i, part in enumerate(parts):
            slots[i * 16 // len(parts)].append(part)

        def between(i):
            for part in slots[i]:
                part()

        factor_block(k, a_s, s_s, e_s, u_s, inv_s, low_s, between)
        return carry

    lax.fori_loop(0, 4, block_body, 0)

    inverses = [pair_inverse(p, inv_s, low_s) for p in range(2)]
    cross = split(jnp.concatenate([u_s[0, :, HALF:], u_s[1, :, BLOCK : BLOCK + HALF]], 0))
    rows_gram = (gr_in[...] + (gr[0] + gr[1])) + ((gr[2] + gr[3]) + (gr[4] + gr[5]))
    rows_gram = rows_gram + diagonal(rows_gram.shape, first_row, 0, ridge_panel[...])
    solve_rows(rows_gram, inverses, cross, pr)
    solve_rows(gc, inverses, cross, pc)

    rows, cols = tile_out.shape
    total = gt[...]
    ri = first_row + lax.broadcasted_iota(jnp.int32, total.shape, 0)
    ci = first_col + lax.broadcasted_iota(jnp.int32, total.shape, 1)
    update = dot3(split(pr[...]), split(pc[...]))
    total = jnp.where((ri >= PANEL) & (ci >= PANEL), total - update, total)
    tile_out[...] = total[0:rows, 0:cols]
    line = first_row + lax.broadcasted_iota(jnp.int32, (rows, PANEL), 0)
    at = lax.broadcasted_iota(jnp.int32, (rows, PANEL), 1)
    rows_out[...] = jnp.where(at <= line, pr[0:rows, :], 0.0)


def main(scal, own, oth_a, oth_b, oth, tables, ridge_panel, sums, rows, cols, scale):
    modes, n = own.shape[1:]
    lr, rr, lc, rc = tables
    row_pad, col_pad = lr.shape[0], lc.shape[0]
    vmem = pl.BlockSpec(memory_space=pltpu.VMEM)
    return pl.pallas_call(
        functools.partial(main_kernel, modes, scale),
        in_specs=[pl.BlockSpec(memory_space=pltpu.SMEM)] + [vmem] * 14,
        out_specs=[vmem, vmem],
        out_shape=[jax.ShapeDtypeStruct((rows, cols), F32), jax.ShapeDtypeStruct((rows, PANEL), F32)],
        scratch_shapes=[
            pltpu.VMEM((LATE, modes, n), F32),
            pltpu.VMEM((2, PANEL, n), F32),
            pltpu.VMEM((LATE, PANEL, n), BF16),
            pltpu.VMEM((LATE, PANEL, n), BF16),
            pltpu.VMEM((4, PANEL, PANEL), F32),
            pltpu.VMEM((PANEL, PANEL), F32),
            pltpu.VMEM((BLOCK, 2 * BLOCK), F32),
            pltpu.VMEM((BLOCK, BLOCK), F32),
            pltpu.VMEM((4, BLOCK, PANEL), F32),
            pltpu.VMEM((4, BLOCK, BLOCK), F32),
            pltpu.VMEM((4, BLOCK, BLOCK), F32),
            pltpu.VMEM((LATE // 2, row_pad, PANEL), F32),
            pltpu.VMEM((col_pad, PANEL), F32),
            pltpu.VMEM((row_pad, col_pad), F32),
            pltpu.VMEM((row_pad, PANEL), F32),
            pltpu.VMEM((col_pad, PANEL), F32),
        ],
        compiler_params=pltpu.CompilerParams(vmem_limit_bytes=44 * 2**20),
        name="gram_factor",
    )(scal, own, oth_a, oth_b, oth, lr, rr, lc, rc, ridge_panel, *sums)


def swap(value, axis, bit):
    size = lax.axis_size(axis)
    return lax.ppermute(value, axis, [(i, i ^ bit) for i in range(size)])


def padded(count):
    return -(-count // 16) * 16


def per_device(snapshots, pod_basis, reference_field, ridge_weights):
    contract = (((1,), (1,)), ((), ()))
    modes = pod_basis.shape[0]
    snap_total = snapshots.shape[0] * lax.axis_size("snap")
    scale = snap_total**-0.5
    feature_total = ridge_weights.shape[0]
    rows = feature_total // lax.axis_size("cells")
    cols = feature_total // lax.axis_size("snap")
    group = lax.axis_index("snap")
    core = lax.axis_index("cells") & 1
    first_row = lax.axis_index("cells") * rows
    first_col = group * cols
    scal = jnp.stack([first_row, first_col]).astype(jnp.int32)
    tables = picks(scal, padded(rows), padded(cols), modes, scale)
    ridge_panel = ridge_weights[None, :PANEL]
    ridge_cols = lax.dynamic_slice_in_dim(ridge_weights, first_col, cols)
    ridge_cols = jnp.pad(ridge_cols, (0, padded(cols) - cols))[None, :]

    projected = lax.dot_general(pod_basis, snapshots, contract, preferred_element_type=F32)
    offset = lax.dot_general(pod_basis, reference_field[None, :], contract, preferred_element_type=F32)
    partial = projected - offset

    half = partial.shape[1] // 2
    keep = lax.dynamic_slice_in_dim(partial, core * half, half, 1)
    send = lax.dynamic_slice_in_dim(partial, (1 - core) * half, half, 1)
    total = keep + swap(send, "cells", 1)
    for bit in (2, 4, 8):
        total = total + swap(total, "cells", bit)

    together = lax.optimization_barrier
    own0 = total[None]
    own1 = swap(own0, "snap", 4)
    oth0 = swap(own0, "cells", 1)
    own1, oth0, tables, ridge_panel, ridge_cols = together((own1, oth0, tables, ridge_panel, ridge_cols))
    pair = jnp.concatenate([own0, own1], 0)
    own2 = swap(pair, "snap", 2)
    oth_pair = jnp.concatenate([oth0, swap(own1, "cells", 1)], 0)
    sums = early(pair, oth_pair, tables, (scal, ridge_panel, ridge_cols), True, modes, scale, 2 * 10**9)
    own2, oth_pair, a0, gr, gc, gt = together((own2, oth_pair, *sums))
    own3 = swap(jnp.concatenate([pair, own2], 0), "snap", 1)
    oth2 = swap(own2, "cells", 1)
    sums = early(own2, oth2, tables, (gr, gc, gt), False, modes, scale, 2 * 10**9)
    own3, oth2, a1, gr, gc, gt = together((own3, oth2, *sums))
    oth3 = swap(own3, "cells", 1)
    sums = (a0, a1, gr, gc, gt)
    return tuple(main(scal, own3, oth_pair, oth2, oth3, tables, ridge_panel, sums, rows, cols, scale))


def solution(mesh):
    return jax.shard_map(
        per_device,
        mesh=mesh,
        in_specs=(P("snap", "cells"), P(None, "cells"), P("cells"), P()),
        out_specs=(P("cells", "snap"), P("cells", None)),
        check_vma=False,
    )
```

time: 102 us -> 84.5 us (0.83)
  waiting for transfers between devices: 20.7 us -> 11.9 us
  Pallas kernels: 47.5 us -> 42.2 us
  local copies, waits for them, and re-layouts: 7.47 us -> 2.64 us
  starting transfers between devices: 20.6 us -> 22.7 us
    ppermute x8 -> x11, waiting for transfers between devices: 20.7 us -> 11.9 us  [swap(): return lax.ppermute(value, axis, [(i, i ^ bit) for i in range(size)])]
    pallas_call x2 -> x4, Pallas kernels: 47.5 us -> 42.2 us  [the longest x1 32.1 us: main(): pl.pallas_call(functools.partial(main_kernel, modes, scale), in_specs=[pl...]
    unnamed x17 -> x4, local copies, waits for them, and re-layouts: 4.81 us -> 1.14 us
    ppermute x8 -> x11, starting transfers between devices: 20.6 us -> 22.7 us  [swap(): return lax.ppermute(value, axis, [(i, i ^ bit) for i in range(size)])]
  transfers between devices with their start and end apart: 8 -> 11, of which waited for: 7 -> 8; matrix products, arithmetic and copies ran while one was open for 3% -> 2% of each run, Pallas kernels for 1% -> 12%
where the time goes in v1:
time: 84.5 us; the launch traced here: 84.3 us
  Pallas kernels  42.2 us (50%)
  starting transfers between devices  22.7 us (27%)
  waiting for transfers between devices  11.9 us (14%)
  matrix products  3.93 us (5%)
  local copies, waits for them, and re-layouts  2.64 us (3%)
    pallas_call x1, Pallas kernels, main(): pl.pallas_call(functools.partial(main_kernel, modes, scale), in_specs=[pl...  32.1 us
    ppermute x11, starting transfers between devices, swap(): return lax.ppermute(value, axis, [(i, i ^ bit) for i in range(size)])  22.7 us
    ppermute x11, waiting for transfers between devices, swap(): return lax.ppermute(value, axis, [(i, i ^ bit) for i in range(size)])  11.9 us
    pallas_call x2, Pallas kernels, early(): pl.pallas_call(functools.partial(early_kernel, modes, scale, first, False...  8.92 us
    dot_general x1, matrix products, per_device(): lax.dot_general(pod_basis, snapshots, contract, preferred_element_type=F32)  3.63 us
  transfers between devices with their start and end apart: 11, of which 8 were waited for; matrix products, arithmetic and copies ran while one was open for 2% of the time, Pallas kernels for 12%

profile of v1, /device:TPU:1, one launch (start us, length us, event | category | flops | bytes accessed | tf_op | source)
XLA Modules:
  0.0 84.3 jit_solution(17038173310787999197)
XLA Ops:
  0.7 0.8 reshape.8
  2.1 3.6 %convolution_subtract_fusion = f32[96,512]{1,0:T(8,128)S(1)} fusion(bf16[96,4096]{1,0:T(8,128)(2,1)S(1)} %copy-done, bf16[512,4096]{1,0:T(8,128)(2,1)} %param.4, f32[96]{0:T(128)S(1)} %convolution_bitcast_fusion), kind=kOutput, calls=%fused_computation | convolution fusion | flops 402702336 | bytes 5177728 | tf_op jit(solution)/shard_map/dot_general | solution.py:424
  5.7 1.5 %collective-permute-start = (f32[96,256]{1,0:T(8,128)S(1)}, f32[96,256]{1,0:T(8,128)S(1)}, u32[]{:S(2)}, u32[]{:S(2)}) collective-permute-start(f32[96,256]{1,0:T(8,128)S(1)} %constant_dynamic-slice_fusion), channel_id=1, source_target_pairs={{0,8},{8,0},{16,24},{24,16},{32,40},{40,32},{48,56},{56,48},{64,72... | collective-permute-start | bytes 294920 | tf_op jit(solution)/shard_map/ppermute | solution.py:399
  7.2 0.9 %collective-permute-done = f32[96,256]{1,0:T(8,128)S(1)} collective-permute-done((f32[96,256]{1,0:T(8,128)S(1)}, f32[96,256]{1,0:T(8,128)S(1)}, u32[]{:S(2)}, u32[]{:S(2)}) %collective-permute-start) | collective-permute-done | bytes 98336 | tf_op jit(solution)/shard_map/ppermute | solution.py:399
  8.2 1.5 %collective-permute-start.1 = (f32[96,256]{1,0:T(8,128)S(1)}, f32[96,256]{1,0:T(8,128)S(1)}, u32[]{:S(2)}, u32[]{:S(2)}) collective-permute-start(f32[96,256]{1,0:T(8,128)S(1)} %dynamic-slice_add_fusion), channel_id=1, source_target_pairs={{0,16},{8,24},{16,0},{24,8},{32,48},{40,56},{48,32},{56,40},{64,80... | collective-permute-start | bytes 294920 | tf_op jit(solution)/shard_map/ppermute | solution.py:399
  9.7 2.6 %collective-permute-done.1 = f32[96,256]{1,0:T(8,128)S(1)} collective-permute-done((f32[96,256]{1,0:T(8,128)S(1)}, f32[96,256]{1,0:T(8,128)S(1)}, u32[]{:S(2)}, u32[]{:S(2)}) %collective-permute-start.1) | collective-permute-done | bytes 98336 | tf_op jit(solution)/shard_map/ppermute | solution.py:399
  12.3 1.8 %collective-permute-start.2 = (f32[96,256]{1,0:T(8,128)S(1)}, f32[96,256]{1,0:T(8,128)S(1)}, u32[]{:S(2)}, u32[]{:S(2)}) collective-permute-start(f32[96,256]{1,0:T(8,128)S(1)} %add.26), channel_id=1, source_target_pairs={{0,32},{8,40},{16,48},{24,56},{32,0},{40,8},{48,16},{56,24},{64,96... | collective-permute-start | bytes 294920 | tf_op jit(solution)/shard_map/ppermute | solution.py:399
  14.1 2.0 %collective-permute-done.2 = f32[96,256]{1,0:T(8,128)S(1)} collective-permute-done((f32[96,256]{1,0:T(8,128)S(1)}, f32[96,256]{1,0:T(8,128)S(1)}, u32[]{:S(2)}, u32[]{:S(2)}) %collective-permute-start.2) | collective-permute-done | bytes 98336 | tf_op jit(solution)/shard_map/ppermute | solution.py:399
  16.2 3.5 %collective-permute-start.3 = (f32[96,256]{1,0:T(8,128)S(1)}, f32[96,256]{1,0:T(8,128)S(1)}, u32[]{:S(2)}, u32[]{:S(2)}) collective-permute-start(f32[96,256]{1,0:T(8,128)S(1)} %add.27), channel_id=1, source_target_pairs={{0,64},{8,72},{16,80},{24,88},{32,96},{40,104},{48,112},{56,120},{... | collective-permute-start | bytes 294920 | tf_op jit(solution)/shard_map/ppermute | solution.py:399
  21.1 1.0 %collective-permute-done.3 = f32[96,256]{1,0:T(8,128)S(1)} collective-permute-done((f32[96,256]{1,0:T(8,128)S(1)}, f32[96,256]{1,0:T(8,128)S(1)}, u32[]{:S(2)}, u32[]{:S(2)}) %collective-permute-start.3) | collective-permute-done | bytes 98336 | tf_op jit(solution)/shard_map/ppermute | solution.py:399
  22.2 3.0 %collective-permute-start.4 = (f32[1,96,256]{2,1,0:T(8,128)S(1)}, f32[1,96,256]{2,1,0:T(8,128)S(1)}, u32[]{:S(2)}, u32[]{:S(2)}) collective-permute-start(f32[1,96,256]{2,1,0:T(8,128)S(1)} %add_bitcast_fusion), channel_id=1, source_target_pairs={{0,4},{1,5},{2,6},{3,7},{4,0},{5,1},{6,2},{7,3},{8,12},{9,13},{10,... | collective-permute-start | bytes 294920 | tf_op jit(solution)/shard_map/ppermute | solution.py:399
  25.1 3.0 %collective-permute-start.5 = (f32[1,96,256]{2,1,0:T(8,128)S(1)}, f32[1,96,256]{2,1,0:T(8,128)S(1)}, u32[]{:S(2)}, u32[]{:S(2)}) collective-permute-start(f32[1,96,256]{2,1,0:T(8,128)S(1)} %add_bitcast_fusion), channel_id=1, source_target_pairs={{0,8},{8,0},{16,24},{24,16},{32,40},{40,32},{48,56},{56,48},{64,72... | collective-permute-start | bytes 294920 | tf_op jit(solution)/shard_map/ppermute | solution.py:399
  28.2 1.2 %picks.1 = (bf16[304,224]{1,0:T(8,128)(2,1)S(1)}, bf16[304,224]{1,0:T(8,128)(2,1)S(1)}, bf16[608,224]{1,0:T(8,128)(2,1)S(1)}, bf16[608,224]{1,0:T(8,128)(2,1)S(1)}) custom-call(s32[2]{0:T(128)S(1)} %pad_add_fusion.scal.refs_6_), custom_call_target="tpu_custom_call" | custom-call | tf_op jit(solution)/shard_map/picks/pallas_call | solution.py:66
  29.5 1.6 %collective-permute-start.7 = (f32[1,96,256]{2,1,0:T(8,128)S(1)}, f32[1,96,256]{2,1,0:T(8,128)S(1)}, u32[]{:S(2)}, u32[]{:S(2)}) collective-permute-start(f32[1,96,256]{2,1,0:T(8,128)S(1)} %collective-permute-done.4), channel_id=1, source_target_pairs={{0,8},{8,0},{16,24},{24,16},{32,40},{40,32},{48,56},{56,48},{64,72... | collective-permute-start | bytes 294920 | tf_op jit(solution)/shard_map/ppermute | solution.py:399
  31.1 2.8 %collective-permute-start.6 = (f32[2,96,256]{2,1,0:T(8,128)S(1)}, f32[2,96,256]{2,1,0:T(8,128)S(1)}, u32[]{:S(2)}, u32[]{:S(2)}) collective-permute-start(f32[2,96,256]{2,1,0:T(8,128)S(1)} %pad_maximum_fusion.1.refs_0_), channel_id=1, source_target_pairs={{0,2},{1,3},{2,0},{3,1},{4,6},{5,7},{6,4},{7,5},{8,10},{9,11},{10,... | collective-permute-start | bytes 589832 | tf_op jit(solution)/shard_map/ppermute | solution.py:399
  34.0 4.7 %early_first.1 = (f32[512,512]{1,0:T(8,128)S(1)}, f32[304,512]{1,0:T(8,128)S(1)}, f32[608,512]{1,0:T(8,128)S(1)}, f32[304,608]{1,0:T(8,128)S(1)}) custom-call(f32[2,96,256]{2,1,0:T(8,128)S(1)} %pad_maximum_fusion.1.refs_0_, f32[2,96,256]{2,1,0:T(8,128)S(1)} %constant_dynamic-update-slice_fusion.refs_1_.oth_a, ...), custom_call_target="tpu_custom_call" | custom-call | flops 2000000000 | bytes 4194304 | tf_op jit(solution)/shard_map/early_first/pallas_call | solution.py:285
  39.3 1.3 %collective-permute-start.8 = (f32[4,96,256]{2,1,0:T(8,128)S(1)}, f32[4,96,256]{2,1,0:T(8,128)S(1)}, u32[]{:S(2)}, u32[]{:S(2)}) collective-permute-start(f32[4,96,256]{2,1,0:T(8,128)S(1)} %pad_maximum_fusion), channel_id=1, source_target_pairs={{0,1},{1,0},{2,3},{3,2},{4,5},{5,4},{6,7},{7,6},{8,9},{9,8},{10,11... | collective-permute-start | bytes 1179656 | tf_op jit(solution)/shard_map/ppermute | solution.py:399
  40.5 1.1 %collective-permute-start.9 = (f32[2,96,256]{2,1,0:T(8,128)S(1)}, f32[2,96,256]{2,1,0:T(8,128)S(1)}, u32[]{:S(2)}, u32[]{:S(2)}) collective-permute-start(f32[2,96,256]{2,1,0:T(8,128)S(1)} %collective-permute-done.6.refs_0_), channel_id=1, source_target_pairs={{0,8},{8,0},{16,24},{24,16},{32,40},{40,32},{48,56},{56,48},{64,72... | collective-permute-start | bytes 589832 | tf_op jit(solution)/shard_map/ppermute | solution.py:399
  41.6 1.1 %collective-permute-done.9.refs_1_.oth_b = f32[2,96,256]{2,1,0:T(8,128)S(1)} collective-permute-done((f32[2,96,256]{2,1,0:T(8,128)S(1)}, f32[2,96,256]{2,1,0:T(8,128)S(1)}, u32[]{:S(2)}, u32[]{:S(2)}) %collective-permute-start.9) | collective-permute-done | bytes 196640 | tf_op jit(solution)/shard_map/ppermute | solution.py:399
  42.7 4.2 %early_second.1 = (f32[512,512]{1,0:T(8,128)S(1)}, f32[304,512]{1,0:T(8,128)S(1)}, f32[608,512]{1,0:T(8,128)S(1)}, f32[304,608]{1,0:T(8,128)S(1)}) custom-call(f32[2,96,256]{2,1,0:T(8,128)S(1)} %collective-permute-done.6.refs_0_, f32[2,96,256]{2,1,0:T(8,128)S(1)} %collective-permute-done.9.refs_1_.oth_b, bf16[304,224]{1,0:T(8,128)(2,1)S(1)} %get-tuple-element.40.refs_2_.lr, ...), custom_call_target="tpu_custom_call" | custom-call | flops 2000000000 | bytes 4194304 | tf_op jit(solution)/shard_map/early_second/pallas_call | solution.py:285
  46.9 2.3 %collective-permute-done.8.own = f32[4,96,256]{2,1,0:T(8,128)S(1)} collective-permute-done((f32[4,96,256]{2,1,0:T(8,128)S(1)}, f32[4,96,256]{2,1,0:T(8,128)S(1)}, u32[]{:S(2)}, u32[]{:S(2)}) %collective-permute-start.8) | collective-permute-done | bytes 393248 | tf_op jit(solution)/shard_map/ppermute | solution.py:399
  49.2 1.7 %collective-permute-start.10 = (f32[4,96,256]{2,1,0:T(8,128)S(1)}, f32[4,96,256]{2,1,0:T(8,128)S(1)}, u32[]{:S(2)}, u32[]{:S(2)}) collective-permute-start(f32[4,96,256]{2,1,0:T(8,128)S(1)} %collective-permute-done.8.own), channel_id=1, source_target_pairs={{0,8},{8,0},{16,24},{24,16},{32,40},{40,32},{48,56},{56,48},{64,72... | collective-permute-start | bytes 1179656 | tf_op jit(solution)/shard_map/ppermute | solution.py:399
  50.9 1.3 %collective-permute-done.10.oth = f32[4,96,256]{2,1,0:T(8,128)S(1)} collective-permute-done((f32[4,96,256]{2,1,0:T(8,128)S(1)}, f32[4,96,256]{2,1,0:T(8,128)S(1)}, u32[]{:S(2)}, u32[]{:S(2)}) %collective-permute-start.10) | collective-permute-done | bytes 393248 | tf_op jit(solution)/shard_map/ppermute | solution.py:399
  52.2 32.1 %gram_factor.1 = (f32[297,594]{1,0:T(8,128)}, f32[297,512]{1,0:T(8,128)}) custom-call(s32[2]{0:T(128)S(1)} %pad_add_fusion.scal.refs_6_, f32[4,96,256]{2,1,0:T(8,128)S(1)} %collective-permute-done.8.own, f32[2,96,256]{2,1,0:T(8,128)S(1)} %constant_dynamic-update-slice_fusion.refs_1_.oth_a, f32[2,96,256]{2,1,0:T(8,128)S(1)} %collective-permute-done.9.refs_1_.oth_b, ...), custom_call_target="tpu_custom_call" | custom-call | tf_op jit(solution)/shard_map/gram_factor/pallas_call | solution.py:369
  (21 shorter events, 2.9 us)
Async XLA Ops:
  0.6 1.2 %copy-start = (bf16[96,4096]{1,0:T(8,128)(2,1)S(1)}, bf16[96,4096]{1,0:T(8,128)(2,1)}, u32[]{:S(2)}) copy-start(bf16[96,4096]{1,0:T(8,128)(2,1)} %param.5) | copy-start | bytes 2359300
  5.7 2.4 %collective-permute-start = (f32[96,256]{1,0:T(8,128)S(1)}, f32[96,256]{1,0:T(8,128)S(1)}, u32[]{:S(2)}, u32[]{:S(2)}) collective-permute-start(f32[96,256]{1,0:T(8,128)S(1)} %constant_dynamic-slice_fusion), channel_id=1, source_target_pairs={{0,8},{8,0},{16,24},{24,16},{32,40},{40,32},{48,56},{56,48},{64,72... | collective-permute-start | bytes 294920 | tf_op jit(solution)/shard_map/ppermute | solution.py:399
  8.2 4.1 %collective-permute-start.1 = (f32[96,256]{1,0:T(8,128)S(1)}, f32[96,256]{1,0:T(8,128)S(1)}, u32[]{:S(2)}, u32[]{:S(2)}) collective-permute-start(f32[96,256]{1,0:T(8,128)S(1)} %dynamic-slice_add_fusion), channel_id=1, source_target_pairs={{0,16},{8,24},{16,0},{24,8},{32,48},{40,56},{48,32},{56,40},{64,80... | collective-permute-start | bytes 294920 | tf_op jit(solution)/shard_map/ppermute | solution.py:399
  12.3 3.8 %collective-permute-start.2 = (f32[96,256]{1,0:T(8,128)S(1)}, f32[96,256]{1,0:T(8,128)S(1)}, u32[]{:S(2)}, u32[]{:S(2)}) collective-permute-start(f32[96,256]{1,0:T(8,128)S(1)} %add.26), channel_id=1, source_target_pairs={{0,32},{8,40},{16,48},{24,56},{32,0},{40,8},{48,16},{56,24},{64,96... | collective-permute-start | bytes 294920 | tf_op jit(solution)/shard_map/ppermute | solution.py:399
  16.2 6.0 %collective-permute-start.3 = (f32[96,256]{1,0:T(8,128)S(1)}, f32[96,256]{1,0:T(8,128)S(1)}, u32[]{:S(2)}, u32[]{:S(2)}) collective-permute-start(f32[96,256]{1,0:T(8,128)S(1)} %add.27), channel_id=1, source_target_pairs={{0,64},{8,72},{16,80},{24,88},{32,96},{40,104},{48,112},{56,120},{... | collective-permute-start | bytes 294920 | tf_op jit(solution)/shard_map/ppermute | solution.py:399
  22.2 7.3 %collective-permute-start.4 = (f32[1,96,256]{2,1,0:T(8,128)S(1)}, f32[1,96,256]{2,1,0:T(8,128)S(1)}, u32[]{:S(2)}, u32[]{:S(2)}) collective-permute-start(f32[1,96,256]{2,1,0:T(8,128)S(1)} %add_bitcast_fusion), channel_id=1, source_target_pairs={{0,4},{1,5},{2,6},{3,7},{4,0},{5,1},{6,2},{7,3},{8,12},{9,13},{10,... | collective-permute-start | bytes 294920 | tf_op jit(solution)/shard_map/ppermute | solution.py:399
  25.1 4.3 %collective-permute-start.5 = (f32[1,96,256]{2,1,0:T(8,128)S(1)}, f32[1,96,256]{2,1,0:T(8,128)S(1)}, u32[]{:S(2)}, u32[]{:S(2)}) collective-permute-start(f32[1,96,256]{2,1,0:T(8,128)S(1)} %add_bitcast_fusion), channel_id=1, source_target_pairs={{0,8},{8,0},{16,24},{24,16},{32,40},{40,32},{48,56},{56,48},{64,72... | collective-permute-start | bytes 294920 | tf_op jit(solution)/shard_map/ppermute | solution.py:399
  29.5 4.5 %collective-permute-start.7 = (f32[1,96,256]{2,1,0:T(8,128)S(1)}, f32[1,96,256]{2,1,0:T(8,128)S(1)}, u32[]{:S(2)}, u32[]{:S(2)}) collective-permute-start(f32[1,96,256]{2,1,0:T(8,128)S(1)} %collective-permute-done.4), channel_id=1, source_target_pairs={{0,8},{8,0},{16,24},{24,16},{32,40},{40,32},{48,56},{56,48},{64,72... | collective-permute-start | bytes 294920 | tf_op jit(solution)/shard_map/ppermute | solution.py:399
  31.1 8.1 %collective-permute-start.6 = (f32[2,96,256]{2,1,0:T(8,128)S(1)}, f32[2,96,256]{2,1,0:T(8,128)S(1)}, u32[]{:S(2)}, u32[]{:S(2)}) collective-permute-start(f32[2,96,256]{2,1,0:T(8,128)S(1)} %pad_maximum_fusion.1.refs_0_), channel_id=1, source_target_pairs={{0,2},{1,3},{2,0},{3,1},{4,6},{5,7},{6,4},{7,5},{8,10},{9,11},{10,... | collective-permute-start | bytes 589832 | tf_op jit(solution)/shard_map/ppermute | solution.py:399
  39.3 9.9 %collective-permute-start.8 = (f32[4,96,256]{2,1,0:T(8,128)S(1)}, f32[4,96,256]{2,1,0:T(8,128)S(1)}, u32[]{:S(2)}, u32[]{:S(2)}) collective-permute-start(f32[4,96,256]{2,1,0:T(8,128)S(1)} %pad_maximum_fusion), channel_id=1, source_target_pairs={{0,1},{1,0},{2,3},{3,2},{4,5},{5,4},{6,7},{7,6},{8,9},{9,8},{10,11... | collective-permute-start | bytes 1179656 | tf_op jit(solution)/shard_map/ppermute | solution.py:399
  40.5 2.1 %collective-permute-start.9 = (f32[2,96,256]{2,1,0:T(8,128)S(1)}, f32[2,96,256]{2,1,0:T(8,128)S(1)}, u32[]{:S(2)}, u32[]{:S(2)}) collective-permute-start(f32[2,96,256]{2,1,0:T(8,128)S(1)} %collective-permute-done.6.refs_0_), channel_id=1, source_target_pairs={{0,8},{8,0},{16,24},{24,16},{32,40},{40,32},{48,56},{56,48},{64,72... | collective-permute-start | bytes 589832 | tf_op jit(solution)/shard_map/ppermute | solution.py:399
  49.2 3.0 %collective-permute-start.10 = (f32[4,96,256]{2,1,0:T(8,128)S(1)}, f32[4,96,256]{2,1,0:T(8,128)S(1)}, u32[]{:S(2)}, u32[]{:S(2)}) collective-permute-start(f32[4,96,256]{2,1,0:T(8,128)S(1)} %collective-permute-done.8.own), channel_id=1, source_target_pairs={{0,8},{8,0},{16,24},{24,16},{32,40},{40,32},{48,56},{56,48},{64,72... | collective-permute-start | bytes 1179656 | tf_op jit(solution)/shard_map/ppermute | solution.py:399
